TPU v7x, 32 devices: a whole 2x2x4 slice. The times are simulated.
32 devices in a mesh: shot: 2 (over y), freq: 8 (over z, x), field: 2 (over core).
Axes of the slice: x: 2, y: 2, z: 4, core: 2. Of those that a mesh axis runs over, the one named last changes fastest.
Arguments:
- traces: bfloat16 [2, 1024, 32, 256], P('field', None, ('shot', 'freq')), parts along dimension 2, may hold values from -6 to 6
- slowness: float32 [4, 16, 256], P('shot', 'freq'), parts along dimension 0, may hold values from 0.4 to 1
Outputs:
- image: float32 [32, 2, 16, 256], P(('shot', 'freq'), None, 'field'), parts along dimension 0
There are 2 independent parts, one for each index of `shot`. A program takes and returns all parts, laid end to end along the dimension named above; each array names one. Nothing has to cross between parts.
All inputs are finite; a program needn't handle non-finite values.
Results may differ from a plain program's by a relative error of at most 0.0032.
Values sent between devices are 32-bit elements; how exact they have to be, the bound alone decides.
A program may use at most 64 MiB of HBM per device.

v0:
```python
import math

import jax
import jax.numpy as jnp
from jax import lax
from jax.sharding import PartitionSpec as P

NT = 1024
FDEV = 2
DEPTHS = 2
NTERMS = 12
NODES = 16


lowest_bin = 8
top_wavenumber = 3.0


def dft_table(bin_count, length):
    freq_bins = lowest_bin + jnp.arange(bin_count, dtype=jnp.int32)
    samples = jnp.arange(length, dtype=jnp.int32)
    phases = freq_bins[:, None] * samples[None, :] % length
    angles = phases.astype(jnp.float32) * (2.0 * math.pi / length)
    norm_scale = 1.0 / math.sqrt(length)
    return jnp.concatenate(
        [jnp.cos(angles) * norm_scale, -jnp.sin(angles) * norm_scale], axis=0
    ).astype(jnp.bfloat16)


def coefficients(slow_plane, freq_bins, bin_count):
    node_angles = (jnp.arange(NODES, dtype=jnp.float32) + 0.5) * (math.pi / NODES)
    term_order = jnp.arange(NTERMS, dtype=jnp.float32)
    weights = jnp.cos(node_angles[:, None] * term_order[None, :]) * (2.0 / NODES)
    weights = weights * jnp.where(term_order == 0, 0.5, 1.0)[None, :]
    wavenumber = (
        top_wavenumber * freq_bins[:, None, None] / (lowest_bin + bin_count) * slow_plane[None]
    )
    depart = wavenumber[None] ** 2 - (node_angles**2)[:, None, None, None]
    travel = jnp.sqrt(jnp.maximum(depart, 0.0))
    amplitude = jnp.exp(-jnp.sqrt(jnp.maximum(-depart, 0.0)))
    real_part = amplitude * jnp.cos(travel)
    imag_part = amplitude * jnp.sin(travel)
    real_coef = jnp.einsum("jn,jfxy->nfxy", weights, real_part, precision=lax.Precision.HIGHEST)
    imag_coef = jnp.einsum("jn,jfxy->nfxy", weights, imag_part, precision=lax.Precision.HIGHEST)
    return (real_coef, imag_coef)


def shift_rows(values):
    padded = jnp.pad(values, [(0, 0)] * (values.ndim - 2) + [(1, 1), (0, 0)])
    return 0.5 * (padded[..., 2:, :] + padded[..., :-2, :])


def shift_cols(values):
    padded = jnp.pad(values, [(0, 0)] * (values.ndim - 1) + [(1, 1)])
    return 0.5 * (padded[..., 2:] + padded[..., :-2])


def lateral(values):
    along_rows = shift_rows(values)
    return 0.5 * (along_rows + shift_cols(values) + shift_cols(along_rows) - values)


def extrapolate(wavefield, real_coef, imag_coef, conj_sign):

    def add_term(summed, term_field, position):
        real_c = lax.dynamic_index_in_dim(real_coef, position, 0, keepdims=False)
        imag_c = conj_sign * lax.dynamic_index_in_dim(imag_coef, position, 0, keepdims=False)
        product = jnp.stack(
            [
                real_c * term_field[0] - imag_c * term_field[1],
                real_c * term_field[1] + imag_c * term_field[0],
            ]
        )
        return summed + product

    first_term = lateral(wavefield)
    summed = add_term(jnp.zeros_like(wavefield), wavefield, 0)
    summed = add_term(summed, first_term, 1)

    def advance(position, state):
        previous, current, summed = state
        following = 2.0 * lateral(current) - previous
        return (current, following, add_term(summed, following, position))

    state = lax.fori_loop(2, NTERMS, advance, (wavefield, first_term, summed))
    return state[2]


def correlate(wavefield):
    received = lax.all_to_all(wavefield[None], "field", split_axis=3, concat_axis=0, tiled=True)
    return received[0, 0] * received[1, 0] + received[0, 1] * received[1, 1]


def local(traces, slowness):
    total_bins = FDEV * lax.axis_size("freq")
    dft_rows = dft_table(total_bins, NT)
    local_traces = traces[0]
    rows_here = local_traces.shape[1]
    grid_cols = local_traces.shape[2]
    flat_traces = local_traces.reshape(NT, rows_here * grid_cols)
    spectrum = jnp.dot(dft_rows, flat_traces, preferred_element_type=jnp.float32).reshape(
        2, total_bins, rows_here, grid_cols
    )
    own_spectrum = lax.all_to_all(spectrum, "freq", split_axis=1, concat_axis=2, tiled=True)
    first_bin = lowest_bin + lax.axis_index("freq") * FDEV
    freq_bins = (first_bin + jnp.arange(FDEV, dtype=jnp.int32)).astype(jnp.float32)
    field_side = lax.axis_index("field")
    conj_sign = 1.0 - 2.0 * field_side.astype(jnp.float32)
    whole_model = lax.all_gather(slowness, "freq", axis=1, tiled=True)
    images = []
    wavefield = own_spectrum
    for depth_step in range(DEPTHS):
        slow_plane = whole_model[depth_step]
        real_coef, imag_coef = coefficients(slow_plane, freq_bins, total_bins)
        wavefield = extrapolate(wavefield, real_coef, imag_coef, conj_sign)
        images.append(correlate(wavefield))
    return jnp.stack(images, axis=1)


def solution(mesh):
    return jax.shard_map(
        local,
        mesh=mesh,
        in_specs=(P("field", None, ("shot", "freq"), None), P("shot", "freq", None)),
        out_specs=P(("shot", "freq"), None, "field", None),
        check_vma=False,
    )
```

profile of v0, /device:TPU:0, one launch (start us, length us, event | category | flops | bytes accessed | tf_op | source)
XLA Modules:
  0.0 68.4 jit_solution(14921517486970964092)
XLA Ops:
  0.0 0.3 multiply_convert_fusion.1
  0.4 1.5 %copy.93 = bf16[128,8,2,256]{3,1,2,0:T(8,128)(2,1)S(1)} copy(bf16[128,8,2,256]{3,2,1,0:T(2,128)(2,1)} %bitcast.59) | data formatting | bytes 2097152
  1.8 0.5 copy.65
  2.4 0.4 fusion.112
  2.8 0.7 %copy.66 = f32[2,16,2,256]{3,2,0,1:T(2,128)} copy(f32[2,16,2,256]{3,1,2,0:T(8,128)S(1)} %fusion.112) | data formatting | bytes 131072 | tf_op jit(solution)/shard_map/dot_general | solution.py:101
  3.5 7.3 %all-to-all-start = ((f32[2,16,2,256]{3,2,0,1:T(2,128)}), f32[2,16,2,256]{3,2,0,1:T(2,128)S(1)}, u32[]{:S(2)}, u32[]{:S(2)}) async-start(f32[2,16,2,256]{3,2,0,1:T(2,128)} %copy.66), calls=%async_computation | async-start | bytes 131072 | tf_op jit(solution)/shard_map/all_to_all | solution.py:104
  10.7 0.0 copy-start
  10.8 0.7 copy-done
  11.4 31.0 %all_gather.3 = f32[2,16,256]{2,0,1:T(2,128)S(1)} all-gather(f32[2,2,256]{2,0,1:T(2,128)S(1)} %copy.68), channel_id=1, replica_groups=mesh['shot'=2,'freq'=8,'field'=2] {'freq'}, dimensions={1}, use_global_device_ids=true | all-gather | bytes 36864 | tf_op jit(solution)/shard_map/all_gather | solution.py:109
  42.4 0.1 multiply_multiply_fusion
  42.5 2.6 %fusion.26 = f32[12,2,16,256]{3,0,2,1:T(8,128)S(1)} fusion(f32[16]{0:T(128)S(1)} %get-tuple-element.576, f32[2,16,256]{2,1,0:T(8,128)S(1)} %get-tuple-element.570, f32[12]{0:T(128)S(1)} %fusion.104, f32[16]{0:T(128)S(1)} %get-tuple-element.575), kind=kOutput, calls=%fused_computation.50 | convolution fusion | flops 19661184 | bytes 426160 | tf_op jit(solution)/shard_map/jn,jfxy->nfxy/dot_general | solution.py:43
  45.1 2.6 %fusion.28 = f32[12,2,16,256]{3,0,2,1:T(8,128)S(1)} fusion(f32[16]{0:T(128)S(1)} %get-tuple-element.576, f32[2,16,256]{2,1,0:T(8,128)S(1)} %get-tuple-element.570, f32[12]{0:T(128)S(1)} %fusion.104, f32[16]{0:T(128)S(1)} %get-tuple-element.575), kind=kOutput, calls=%fused_computation.51 | convolution fusion | flops 19661184 | bytes 426160 | tf_op jit(solution)/shard_map/jn,jfxy->nfxy/dot_general | solution.py:44
  47.8 2.6 %fusion.41 = f32[12,2,16,256]{3,0,2,1:T(8,128)S(1)} fusion(f32[2,16,256]{2,1,0:T(8,128)S(1)} %get-tuple-element.569, f32[16]{0:T(128)S(1)} %get-tuple-element.576, f32[12]{0:T(128)S(1)} %fusion.104, f32[16]{0:T(128)S(1)} %get-tuple-element.575), kind=kOutput, calls=%fused_computation.61 | convolution fusion | flops 19661184 | bytes 426160 | tf_op jit(solution)/shard_map/jn,jfxy->nfxy/dot_general | solution.py:43
  50.4 2.6 %fusion.43 = f32[12,2,16,256]{3,0,2,1:T(8,128)S(1)} fusion(f32[2,16,256]{2,1,0:T(8,128)S(1)} %get-tuple-element.569, f32[16]{0:T(128)S(1)} %get-tuple-element.576, f32[12]{0:T(128)S(1)} %fusion.104, f32[16]{0:T(128)S(1)} %get-tuple-element.575), kind=kOutput, calls=%fused_computation.62 | convolution fusion | flops 19661184 | bytes 426160 | tf_op jit(solution)/shard_map/jn,jfxy->nfxy/dot_general | solution.py:44
  53.1 0.2 copy.69
  53.3 0.2 copy.70
  53.5 0.2 copy.77
  53.8 0.2 copy.78
  54.0 0.0 all-to-all-done
  54.1 0.1 fusion.72
  54.4 2.7 %while.42 = (s32[]{:T(128)}, f32[2,2,16,256]{3,2,1,0:T(8,128)S(1)}, f32[2,2,16,256]{3,2,1,0:T(8,128)S(1)}, f32[2,2,16,256]{3,2,1,0:T(8,128)S(1)}, f32[12,2,16,25...) while((s32[]{:T(128)}, f32[2,2,16,256]{3,2,1,0:T(8,128)S(1)}, ...), condition=%wide.region_1.2_spmd, body=%wide.region_0.1_spmd.sunk | while | flops 253958 | bytes 1048747 | solution.py:85
  54.4 0.1 fusion.120
  54.7 0.1 fusion.120
  55.0 0.1 fusion.120
  55.3 0.1 fusion.120
  55.5 0.1 fusion.120
  55.8 0.1 fusion.120
  56.1 0.1 fusion.120
  56.3 0.1 fusion.120
  56.6 0.1 fusion.120
  56.9 0.1 fusion.120
  57.1 0.1 copy.104
  57.2 0.1 fusion.82
  57.4 2.7 %while.43 = (s32[]{:T(128)}, f32[2,2,16,256]{3,2,1,0:T(8,128)S(1)}, f32[2,2,16,256]{3,2,1,0:T(8,128)S(1)}, f32[2,2,16,256]{3,2,1,0:T(8,128)S(1)}, f32[12,2,16,25...) while((s32[]{:T(128)}, f32[2,2,16,256]{3,2,1,0:T(8,128)S(1)}, ...), condition=%wide.region_3.4_spmd, body=%wide.region_2.3_spmd.sunk | while | flops 253958 | bytes 1048747 | solution.py:85
  57.4 0.1 fusion.122
  57.7 0.1 fusion.122
  58.0 0.1 fusion.122
  58.2 0.1 fusion.122
  58.5 0.1 fusion.122
  58.8 0.1 fusion.122
  59.1 0.1 fusion.122
  59.3 0.1 fusion.122
  59.6 0.1 fusion.122
  59.9 0.1 fusion.122
  60.1 0.1 copy.102
  60.2 3.8 %all_to_all.54 = f32[1,2,2,16,256]{4,2,1,0,3:T(2,128)S(1)} all-to-all(f32[1,2,2,16,256]{4,2,1,0,3:T(2,128)S(1)} %bitcast.67), channel_id=1, replica_groups=mesh['shot'=2,'freq'=8,'field'=2] {'field'}, dimensions={3} | all-to-all | bytes 131072 | tf_op jit(solution)/shard_map/all_to_all | solution.py:90
  64.0 3.8 %all_to_all.55 = f32[1,2,2,16,256]{4,2,1,0,3:T(2,128)S(1)} all-to-all(f32[1,2,2,16,256]{4,2,1,0,3:T(2,128)S(1)} %bitcast.65), channel_id=1, replica_groups=mesh['shot'=2,'freq'=8,'field'=2] {'field'}, dimensions={3} | all-to-all | bytes 131072 | tf_op jit(solution)/shard_map/all_to_all | solution.py:90
  67.8 0.6 copy.86
  (124 shorter events, 1.7 us)
Async XLA Ops:
  3.5 50.6 %all-to-all-start = ((f32[2,16,2,256]{3,2,0,1:T(2,128)}), f32[2,16,2,256]{3,2,0,1:T(2,128)S(1)}, u32[]{:S(2)}, u32[]{:S(2)}) async-start(f32[2,16,2,256]{3,2,0,1:T(2,128)} %copy.66), calls=%async_computation | async-start | bytes 131072 | tf_op jit(solution)/shard_map/all_to_all | solution.py:104
  10.7 0.7 %copy-start = (f32[2,2,256]{2,1,0:T(2,128)S(1)}, f32[2,2,256]{2,1,0:T(2,128)}, u32[]{:S(2)}) copy-start(f32[2,2,256]{2,1,0:T(2,128)} %param.7) | copy-start | bytes 12292
where the time goes:
time: 68.8 us; the launch traced here: 68.4 us
  blocking collectives  38.5 us (56%)
  matrix products  10.9 us (16%)
  starting transfers between devices  7.25 us (11%)
  local copies, waits for them, and re-layouts  5.41 us (8%)
  other arithmetic  4.7 us (7%)
  loops' own time  1.3 us (2%)
    all_gather x1, blocking collectives, local(): whole_model = lax.all_gather(slowness, 'freq', axis=1, tiled=True)  31 us
    all_to_all x2, blocking collectives, correlate(): lax.all_to_all(wavefield[None], 'field', split_axis=3, concat_axis=0, til...  7.58 us
    all_to_all x1, starting transfers between devices, local(): lax.all_to_all(spectrum, 'freq', split_axis=1, concat_axis=2, tiled=True)  7.25 us
    dot_general x2, matrix products, coefficients(): jnp.einsum('jn,jfxy->nfxy', weights, imag_part, precision=lax.Precision.H...  5.28 us
    dot_general x2, matrix products, coefficients(): jnp.einsum('jn,jfxy->nfxy', weights, real_part, precision=lax.Precision.H...  5.24 us
    sub x20, other arithmetic, advance(): following = 2.0 * lateral(current) - previous  2.73 us
    unnamed x5, local copies, waits for them, and re-layouts  2.11 us
  transfers between devices with their start and end apart: 1, of which 0 were waited for; matrix products, arithmetic and copies ran while one was open for 17% of the time, Pallas kernels for 0%

commit v1 on v0

v1 whole, which is shorter than its diff:
```python
import functools
import math

import jax
import jax.numpy as jnp
import numpy as np
from jax import lax
from jax.experimental import pallas as pl
from jax.experimental.pallas import tpu as pltpu
from jax.sharding import PartitionSpec as P

NTERMS = 12
NODES = 16
LANES = 128
SUBLANES = 8

lowest_bin = 8
top_wavenumber = 3.0


def dft_rows(bin_count, length, peers, cores, rows_here):
    bins = lowest_bin + np.arange(bin_count)
    samples = np.arange(length)
    angles = (bins[:, None] * samples[None, :] % length).astype(np.float64) * (2.0 * math.pi / length)
    norm_scale = 1.0 / math.sqrt(length)
    table = np.stack([np.cos(angles) * norm_scale, -np.sin(angles) * norm_scale], axis=1)
    table = table.astype(np.float32).astype(jnp.bfloat16)
    spread = np.zeros((bin_count, 2, rows_here, length, rows_here), dtype=jnp.bfloat16)
    for row in range(rows_here):
        spread[:, :, row, :, row] = table
    return spread.reshape(bin_count * 2 * rows_here, length * rows_here)


def power_series(function, degree):
    reach = top_wavenumber**2
    nodes = 0.5 * reach * (1.0 + np.cos(np.pi * (np.arange(64) + 0.5) / 64))
    fitted = np.polynomial.Chebyshev.fit(nodes, function(np.sqrt(nodes)), degree, domain=[0.0, reach])
    return [float(c) for c in fitted.convert(kind=np.polynomial.Polynomial).coef]


COS_SERIES = power_series(np.cos, 6)
SINC_SERIES = power_series(lambda s: np.sin(s) / s, 5)
NODE_ANGLES = [math.pi * (j + 0.5) / NODES for j in range(NODES)]


def horner(series, at):
    value = series[-1] * at + series[-2]
    for factor in series[-3::-1]:
        value = value * at + factor
    return value


def node_value(squared, angle):
    depart = squared - angle * angle
    size = jnp.maximum(jnp.abs(depart), 1e-30)
    root = size * lax.rsqrt(size)
    travels = depart >= 0.0
    real_part = jnp.where(travels, horner(COS_SERIES, depart), jnp.exp(-root))
    imag_part = jnp.where(travels, root * horner(SINC_SERIES, depart), 0.0)
    return real_part, imag_part


def weight(term, node):
    return math.cos(term * NODE_ANGLES[node]) * 2.0 / NODES * (0.5 if term == 0 else 1.0)


def project(parts, terms, count):
    if count > 2:
        half = count // 2
        sums = [parts[j] + parts[count - 1 - j] for j in range(half)]
        stride = NODES // count
        even = [t for t in terms if (t // stride) % 2 == 0]
        odd = [t for t in terms if (t // stride) % 2 == 1]
        found = project(sums, even, half)
        diffs = [parts[j] - parts[count - 1 - j] for j in range(half)]
        for t in odd:
            found[t] = functools.reduce(
                lambda a, b: a + b, [diffs[j] * weight(t, j) for j in range(half)]
            )
        return found
    return {
        t: functools.reduce(lambda a, b: a + b, [parts[j] * weight(t, j) for j in range(count)])
        for t in terms
    }


def lane_pair_sum(values, lane):
    zero = jnp.zeros_like(values[:, :, :1])
    right = pltpu.roll(values, 1, 4)
    left = pltpu.roll(values, LANES - 1, 4)
    from_left = jnp.where(lane == 0, jnp.concatenate([zero, right[:, :, :-1]], axis=2), right)
    from_right = jnp.where(lane == LANES - 1, jnp.concatenate([left[:, :, 1:], zero], axis=2), left)
    return from_left + from_right


def row_pair_sum(values, row):
    zero = jnp.zeros_like(values[:, :1])
    down = pltpu.roll(values, 1, 3)
    up = pltpu.roll(values, SUBLANES - 1, 3)
    from_above = jnp.where(row == 0, jnp.concatenate([zero, down[:, :-1]], axis=1), down)
    from_below = jnp.where(row == SUBLANES - 1, jnp.concatenate([up[:, 1:], zero], axis=1), up)
    return from_above + from_below


def spread_twice(values, lane, row):
    along = values + 0.5 * lane_pair_sum(values, lane)
    return along + 0.5 * row_pair_sum(along, row)


def kernel(
    peers, cores, depths, rows_here, bin_count, cols,
    traces_ref, table_ref, slow_ref, out_ref,
    traces_v, table_v, own_slow, all_slow, send, recv, slow_t, coef, field, image,
    load_sem, slow_send, slow_recv, spec_send, spec_recv, image_send, image_recv,
):
    me = lax.axis_index("freq")
    core = lax.axis_index("field")
    groups = peers * rows_here // SUBLANES
    tiles = cols // LANES
    chunks = groups * tiles

    barrier = pltpu.get_barrier_semaphore()
    others = [(off, turn) for off in range(peers) for turn in range(cores) if (off, turn) != (0, 0)]
    for off, turn in others:
        pl.semaphore_signal(
            barrier, inc=1,
            device_id={"freq": lax.rem(me + off, peers), "field": lax.rem(core + turn, cores)},
            device_id_type=pl.DeviceIdType.MESH,
        )
    load_slow = pltpu.make_async_copy(slow_ref, own_slow, load_sem.at[0])
    load_slow.start()
    load_table = pltpu.make_async_copy(table_ref, table_v, load_sem.at[1])
    load_table.start()
    loads = []
    for t in range(tiles):
        load = pltpu.make_async_copy(
            traces_ref.at[:, :, pl.ds(t * LANES, LANES)], traces_v.at[t], load_sem.at[2 + t]
        )
        load.start()
        loads.append(load)
    load_slow.wait()
    pl.semaphore_wait(barrier, len(others))

    slow_copies = []
    for off in range(1, peers):
        copy = pltpu.make_async_remote_copy(
            src_ref=own_slow, dst_ref=all_slow.at[me],
            send_sem=slow_send.at[off], recv_sem=slow_recv.at[off],
            device_id={"freq": lax.rem(me + off, peers)}, device_id_type=pl.DeviceIdType.MESH,
        )
        copy.start()
        slow_copies.append(copy)
    all_slow[me] = own_slow[...]

    load_table.wait()
    length = traces_v.shape[1]
    for t in range(tiles):
        loads[t].wait()
        block = traces_v[t].reshape(length * rows_here, LANES)
        part = jnp.dot(table_v[...], block, preferred_element_type=jnp.float32)
        send[:, :, :, t * LANES : (t + 1) * LANES] = part.reshape(peers, cores, 2 * rows_here, LANES)

    spec_copies = []
    for number, (off, turn) in enumerate(others):
        peer, side = lax.rem(me + off, peers), lax.rem(core + turn, cores)
        copy = pltpu.make_async_remote_copy(
            src_ref=send.at[peer, side], dst_ref=recv.at[core, me],
            send_sem=spec_send.at[number], recv_sem=spec_recv.at[number],
            device_id={"freq": peer, "field": side}, device_id_type=pl.DeviceIdType.MESH,
        )
        copy.start()
        spec_copies.append(copy)
    recv[core, me] = send[me, core]

    for copy in slow_copies:
        copy.wait()
    for z in range(depths):
        for p in range(peers):
            group, inner = divmod(p * rows_here, SUBLANES)
            for t in range(tiles):
                slow_t[z * chunks + group * tiles + t, inner : inner + rows_here, :] = all_slow[
                    p, z, :, t * LANES : (t + 1) * LANES
                ]

    bin_here = (lowest_bin + me * cores + core).astype(jnp.float32)
    per_slow = top_wavenumber * bin_here / (lowest_bin + bin_count)

    def coefficients(chunk, carry):
        wavenumber = per_slow * slow_t[chunk]
        squared = wavenumber * wavenumber
        pairs = [node_value(squared, angle) for angle in NODE_ANGLES]
        for comp in range(2):
            found = project([pair[comp] for pair in pairs], list(range(NTERMS)), NODES)
            for term in range(NTERMS):
                coef[chunk, 2 * term + comp] = found[term]
        return carry

    lax.fori_loop(0, depths * chunks, coefficients, 0)

    for copy in spec_copies:
        copy.wait()
    for s in range(cores):
        for p in range(peers):
            group, inner = divmod(p * rows_here, SUBLANES)
            for c in range(2):
                for t in range(tiles):
                    field[2 * s + c, group, t, inner : inner + rows_here, :] = recv[
                        s, p, c * rows_here : (c + 1) * rows_here, t * LANES : (t + 1) * LANES
                    ]

    shape = (1, 1, 1, SUBLANES, LANES)
    lane = lax.broadcasted_iota(jnp.int32, shape, 4)
    row = lax.broadcasted_iota(jnp.int32, shape, 3)
    values = field[...]
    half_groups = groups // 2
    image_copies = []
    for z in range(depths):

        def term_of(current, n):
            here = coef[z * chunks : (z + 1) * chunks, pl.ds(2 * n, 2)]
            real_c = here[:, 0].reshape(groups, tiles, SUBLANES, LANES)
            imag_c = here[:, 1].reshape(groups, tiles, SUBLANES, LANES)
            return jnp.stack(
                [
                    real_c * current[0] - imag_c * current[1],
                    real_c * current[1] + imag_c * current[0],
                    real_c * current[2] + imag_c * current[3],
                    real_c * current[3] - imag_c * current[2],
                ]
            )

        first = 0.5 * spread_twice(values, lane, row) - values
        summed = term_of(values, 0) + term_of(first, 1)

        def advance(n, state):
            previous, current, total = state
            following = spread_twice(current, lane, row) - (2.0 * current + previous)
            return current, following, total + term_of(following, n)

        values = lax.fori_loop(
            2, NTERMS, advance, (values, first, summed), unroll=groups <= 4
        )[2]
        picture = values[0] * values[2] + values[1] * values[3]
        for group in range(groups):
            for t in range(tiles):
                image[z, group // half_groups,
                      (group % half_groups) * SUBLANES : (group % half_groups + 1) * SUBLANES,
                      t * LANES : (t + 1) * LANES] = picture[group, t]
        other = lax.rem(core + 1, cores)
        copy = pltpu.make_async_remote_copy(
            src_ref=image.at[z, other], dst_ref=out_ref.at[core, z],
            send_sem=image_send.at[z], recv_sem=image_recv.at[z],
            device_id={"field": other}, device_id_type=pl.DeviceIdType.MESH,
        )
        copy.start()
        image_copies.append(copy)
        out_ref[core, z] = image[z, core]
    for copy in image_copies:
        copy.wait()


def local(traces, slowness):
    peers, cores = lax.axis_size("freq"), lax.axis_size("field")
    _, length, rows_here, cols = traces.shape
    depths = slowness.shape[0]
    bin_count = peers * cores
    table = jnp.asarray(dft_rows(bin_count, length, peers, cores, rows_here))
    grid_rows = peers * rows_here
    groups, tiles = grid_rows // SUBLANES, cols // LANES
    f32 = jnp.float32
    others = peers * cores - 1
    return pl.pallas_call(
        functools.partial(kernel, peers, cores, depths, rows_here, bin_count, cols),
        out_shape=jax.ShapeDtypeStruct((cores, depths, grid_rows // 2, cols), f32),
        in_specs=[pl.BlockSpec(memory_space=pl.ANY)] * 3,
        out_specs=pl.BlockSpec(memory_space=pltpu.VMEM),
        scratch_shapes=[
            pltpu.VMEM((tiles, length, rows_here, LANES), jnp.bfloat16),
            pltpu.VMEM(table.shape, jnp.bfloat16),
            pltpu.VMEM((depths, rows_here, cols), f32),
            pltpu.VMEM((peers, depths, rows_here, cols), f32),
            pltpu.VMEM((peers, cores, 2 * rows_here, cols), f32),
            pltpu.VMEM((cores, peers, 2 * rows_here, cols), f32),
            pltpu.VMEM((depths * groups * tiles, SUBLANES, LANES), f32),
            pltpu.VMEM((depths * groups * tiles, 2 * NTERMS, SUBLANES, LANES), f32),
            pltpu.VMEM((4, groups, tiles, SUBLANES, LANES), f32),
            pltpu.VMEM((depths, 2, grid_rows // 2, cols), f32),
            pltpu.SemaphoreType.DMA((2 + tiles,)),
            pltpu.SemaphoreType.DMA((peers,)),
            pltpu.SemaphoreType.DMA((peers,)),
            pltpu.SemaphoreType.DMA((others,)),
            pltpu.SemaphoreType.DMA((others,)),
            pltpu.SemaphoreType.DMA((depths,)),
            pltpu.SemaphoreType.DMA((depths,)),
        ],
        compiler_params=pltpu.CompilerParams(
            collective_id=0, has_side_effects=True, vmem_limit_bytes=48 * 1024 * 1024
        ),
    )(traces[0], table, slowness)


def solution(mesh):
    return jax.shard_map(
        local,
        mesh=mesh,
        in_specs=(P("field", None, ("shot", "freq"), None), P("shot", "freq", None)),
        out_specs=P(("shot", "freq"), None, "field", None),
        check_vma=False,
    )
```

time: 68.8 us -> 16.8 us (0.24)
  blocking collectives: 38.5 us -> 0 us
  Pallas kernels: 0 us -> 13.2 us
  matrix products: 10.9 us -> 0 us
  starting transfers between devices: 7.25 us -> 0 us
  other arithmetic: 4.7 us -> 0 us
  local copies, waits for them, and re-layouts: 5.41 us -> 3.48 us
  loops' own time: 1.3 us -> 0 us
    all_gather x1 -> x0, blocking collectives: 31 us -> none  [local(): whole_model = lax.all_gather(slowness, 'freq', axis=1, tiled=True)]
    pallas_call x0 -> x1, Pallas kernels: none -> 13.2 us  [local(): pl.pallas_call(functools.partial(kernel, peers, cores, depths, rows_here,...]
    dot_general x5 -> x0, matrix products: 10.9 us -> none  [the longest x2 5.28 us: coefficients(): jnp.einsum('jn,jfxy->nfxy', weights, imag_part, precision=lax.Precision.H...]
    all_to_all x2 -> x0, blocking collectives: 7.58 us -> none  [correlate(): lax.all_to_all(wavefield[None], 'field', split_axis=3, concat_axis=0, til...]
    all_to_all x1 -> x0, starting transfers between devices: 7.25 us -> none  [local(): lax.all_to_all(spectrum, 'freq', split_axis=1, concat_axis=2, tiled=True)]
    sub x42 -> x0, other arithmetic: 3.15 us -> none  [the longest x20 2.73 us: advance(): following = 2.0 * lateral(current) - previous]
    dot_general x6 -> x0, local copies, waits for them, and re-layouts: 2.15 us -> none  [the longest x2 1.22 us: local(): jnp.dot(dft_rows, flat_traces, preferred_element_type=jnp.float32)]
    unnamed x5 -> x7, local copies, waits for them, and re-layouts: 2.11 us -> 3.48 us
  transfers between devices with their start and end apart: 1 -> 0, of which waited for: 0 -> 0; matrix products, arithmetic and copies ran while one was open for 17% -> 0% of each run, Pallas kernels for 0% -> 0%
where the time goes in v1:
time: 16.8 us; the launch traced here: 16.6 us
  Pallas kernels  13.2 us (79%)
  local copies, waits for them, and re-layouts  3.48 us (21%)
    pallas_call x1, Pallas kernels, local(): pl.pallas_call(functools.partial(kernel, peers, cores, depths, rows_here,...  13.2 us
    unnamed x7, local copies, waits for them, and re-layouts  3.48 us

profile of v1, /device:TPU:0, one launch (start us, length us, event | category | flops | bytes accessed | tf_op | source)
XLA Modules:
  0.0 16.6 jit_solution(299943740330905763)
XLA Ops:
  0.0 0.0 copy-start
  0.0 1.2 %copy-done = bf16[1,1024,2,256]{3,2,1,0:T(2,128)(2,1)S(1)} copy-done((bf16[1,1024,2,256]{3,2,1,0:T(2,128)(2,1)S(1)}, bf16[1,1024,2,256]{3,2,1,0:T(2,128)(2,1)}, u32[]{:S(2)}) %copy-start) | copy-done | bytes 1048600
  1.2 0.0 copy-start.1
  1.2 0.9 %copy-done.1 = bf16[64,2048]{1,0:T(8,128)(2,1)S(1)} copy-done((bf16[64,2048]{1,0:T(8,128)(2,1)S(1)}, bf16[64,2048]{1,0:T(8,128)(2,1)}, u32[]{:S(2)}) %copy-start.1) | copy-done | bytes 262168
  2.2 0.0 copy-start.2
  2.2 0.7 %copy-done.2 = f32[2,2,256]{2,1,0:T(2,128)S(1)} copy-done((f32[2,2,256]{2,1,0:T(2,128)S(1)}, f32[2,2,256]{2,1,0:T(2,128)}, u32[]{:S(2)}) %copy-start.2) | copy-done | bytes 4120
  2.9 13.2 %shard_map.37 = f32[2,2,8,256]{3,2,1,0:T(8,128)S(1)} custom-call(bf16[1024,2,256]{2,1,0:T(2,128)(2,1)S(1)} %bitcast.1, bf16[64,2048]{1,0:T(8,128)(2,1)S(1)} %copy-done.1, f32[2,2,256]{2,1,0:T(2,128)S(1)} %copy-done.2), custom_call_target="tpu_custom_call" | custom-call | tf_op jit(solution)/shard_map/pallas_call | solution.py:272
  16.0 0.6 %copy.5 = f32[2,2,8,256]{3,2,1,0:T(8,128)} copy(f32[2,2,8,256]{3,2,1,0:T(8,128)S(1)} %shard_map.37) | data formatting | bytes 65536
Async XLA Ops:
  0.0 1.2 %copy-start = (bf16[1,1024,2,256]{3,2,1,0:T(2,128)(2,1)S(1)}, bf16[1,1024,2,256]{3,2,1,0:T(2,128)(2,1)}, u32[]{:S(2)}) copy-start(bf16[1,1024,2,256]{3,2,1,0:T(2,128)(2,1)} %param.3) | copy-start | bytes 3145732
  1.2 0.9 %copy-start.1 = (bf16[64,2048]{1,0:T(8,128)(2,1)S(1)}, bf16[64,2048]{1,0:T(8,128)(2,1)}, u32[]{:S(2)}) copy-start(bf16[64,2048]{1,0:T(8,128)(2,1)} %constant.2.clone.table_ref) | copy-start | bytes 786436
  2.2 0.7 %copy-start.2 = (f32[2,2,256]{2,1,0:T(2,128)S(1)}, f32[2,2,256]{2,1,0:T(2,128)}, u32[]{:S(2)}) copy-start(f32[2,2,256]{2,1,0:T(2,128)} %slow_ref.1) | copy-start | bytes 12292

commit v2 on v1

--- a/solution.py
+++ b/solution.py
@@ -272,7 +272,7 @@
     return pl.pallas_call(
         functools.partial(kernel, peers, cores, depths, rows_here, bin_count, cols),
         out_shape=jax.ShapeDtypeStruct((cores, depths, grid_rows // 2, cols), f32),
-        in_specs=[pl.BlockSpec(memory_space=pl.ANY)] * 3,
+        in_specs=[pl.BlockSpec(memory_space=pltpu.HBM)] * 3,
         out_specs=pl.BlockSpec(memory_space=pltpu.VMEM),
         scratch_shapes=[
             pltpu.VMEM((tiles, length, rows_here, LANES), jnp.bfloat16),
@@ -294,7 +294,7 @@
             pltpu.SemaphoreType.DMA((depths,)),
         ],
         compiler_params=pltpu.CompilerParams(
-            collective_id=0, has_side_effects=True, vmem_limit_bytes=48 * 1024 * 1024
+            collective_id=0, has_side_effects=True, vmem_limit_bytes=64 * 1024 * 1024
         ),
     )(traces[0], table, slowness)
 

time: 16.8 us -> 15.4 us (0.917)
  local copies, waits for them, and re-layouts: 3.48 us -> 1.38 us
  Pallas kernels: 13.2 us -> 13.8 us
    unnamed x7 -> x1, local copies, waits for them, and re-layouts: 3.48 us -> 1.38 us
    pallas_call x1, Pallas kernels: 13.2 us -> 13.8 us  [local(): pl.pallas_call(functools.partial(kernel, peers, cores, depths, rows_here,...]
where the time goes in v2:
time: 15.4 us; the launch traced here: 15.2 us
  Pallas kernels  13.8 us (90%)
  local copies, waits for them, and re-layouts  1.38 us (9%)
    pallas_call x1, Pallas kernels, local(): pl.pallas_call(functools.partial(kernel, peers, cores, depths, rows_here,...  13.8 us
    unnamed x1, local copies, waits for them, and re-layouts  1.38 us

profile of v2, /device:TPU:0, one launch (start us, length us, event | category | flops | bytes accessed | tf_op | source)
XLA Modules:
  0.0 15.2 jit_solution(577486445549241023)
XLA Ops:
  0.0 13.8 %shard_map.37 = f32[2,2,8,256]{3,2,1,0:T(8,128)} custom-call(bf16[1024,2,256]{2,1,0:T(2,128)(2,1)} %bitcast.1, bf16[64,2048]{1,0:T(8,128)(2,1)} %constant.2.clone.table_ref, f32[2,2,256]{2,1,0:T(2,128)} %slow_ref.1), custom_call_target="tpu_custom_call" | custom-call | tf_op jit(solution)/shard_map/pallas_call | solution.py:272
  13.8 1.4 %copy.5 = f32[2,2,8,256]{3,2,1,0:T(8,128)} copy(f32[2,2,8,256]{3,2,1,0:T(8,128)} %shard_map.37) | data formatting | bytes 65536

commit v3 on v2

--- a/solution.py
+++ b/solution.py
@@ -110,14 +110,16 @@
 def kernel(
     peers, cores, depths, rows_here, bin_count, cols,
     traces_ref, table_ref, slow_ref, out_ref,
-    traces_v, table_v, own_slow, all_slow, send, recv, slow_t, coef, field, image,
-    load_sem, slow_send, slow_recv, spec_send, spec_recv, image_send, image_recv,
+    traces_v, table_v, own_slow, send, recv, slow_t, field, image,
+    load_sem, spec_send, spec_recv, image_send, image_recv, *coef,
 ):
     me = lax.axis_index("freq")
     core = lax.axis_index("field")
     groups = peers * rows_here // SUBLANES
     tiles = cols // LANES
     chunks = groups * tiles
+    inline = chunks <= 4
+    spec_rows = 2 * rows_here
 
     barrier = pltpu.get_barrier_semaphore()
     others = [(off, turn) for off in range(peers) for turn in range(cores) if (off, turn) != (0, 0)]
@@ -127,10 +129,6 @@
             device_id={"freq": lax.rem(me + off, peers), "field": lax.rem(core + turn, cores)},
             device_id_type=pl.DeviceIdType.MESH,
         )
-    load_slow = pltpu.make_async_copy(slow_ref, own_slow, load_sem.at[0])
-    load_slow.start()
-    load_table = pltpu.make_async_copy(table_ref, table_v, load_sem.at[1])
-    load_table.start()
     loads = []
     for t in range(tiles):
         load = pltpu.make_async_copy(
@@ -138,28 +136,27 @@
         )
         load.start()
         loads.append(load)
+    load_table = pltpu.make_async_copy(table_ref, table_v, load_sem.at[1])
+    load_table.start()
+    load_slow = pltpu.make_async_copy(slow_ref, own_slow, load_sem.at[0])
+    load_slow.start()
+
     load_slow.wait()
-    pl.semaphore_wait(barrier, len(others))
-
-    slow_copies = []
-    for off in range(1, peers):
-        copy = pltpu.make_async_remote_copy(
-            src_ref=own_slow, dst_ref=all_slow.at[me],
-            send_sem=slow_send.at[off], recv_sem=slow_recv.at[off],
-            device_id={"freq": lax.rem(me + off, peers)}, device_id_type=pl.DeviceIdType.MESH,
-        )
-        copy.start()
-        slow_copies.append(copy)
-    all_slow[me] = own_slow[...]
-
+    slow_rows = own_slow[...].reshape(depths * rows_here, cols)
+    tail = jnp.concatenate([jnp.zeros((spec_rows, cols), jnp.float32), slow_rows], axis=0)
+    block_row = lax.broadcasted_iota(jnp.int32, (1, 1, 2 * spec_rows, LANES), 2)
     load_table.wait()
     length = traces_v.shape[1]
     for t in range(tiles):
         loads[t].wait()
         block = traces_v[t].reshape(length * rows_here, LANES)
         part = jnp.dot(table_v[...], block, preferred_element_type=jnp.float32)
-        send[:, :, :, t * LANES : (t + 1) * LANES] = part.reshape(peers, cores, 2 * rows_here, LANES)
-
+        part = part.reshape(peers, 1, cores * spec_rows, LANES)
+        both = jnp.concatenate([part, pltpu.roll(part, spec_rows, 2)], axis=1)
+        here = tail[:, t * LANES : (t + 1) * LANES]
+        send[:, :, :, t * LANES : (t + 1) * LANES] = jnp.where(block_row < spec_rows, both, here[None, None])
+
+    pl.semaphore_wait(barrier, len(others))
     spec_copies = []
     for number, (off, turn) in enumerate(others):
         peer, side = lax.rem(me + off, peers), lax.rem(core + turn, cores)
@@ -172,33 +169,16 @@
         spec_copies.append(copy)
     recv[core, me] = send[me, core]
 
-    for copy in slow_copies:
-        copy.wait()
+    for copy in spec_copies:
+        copy.wait_recv()
     for z in range(depths):
         for p in range(peers):
             group, inner = divmod(p * rows_here, SUBLANES)
+            first_row = spec_rows + z * rows_here
             for t in range(tiles):
-                slow_t[z * chunks + group * tiles + t, inner : inner + rows_here, :] = all_slow[
-                    p, z, :, t * LANES : (t + 1) * LANES
+                slow_t[z * chunks + group * tiles + t, inner : inner + rows_here, :] = recv[
+                    0, p, first_row : first_row + rows_here, t * LANES : (t + 1) * LANES
                 ]
-
-    bin_here = (lowest_bin + me * cores + core).astype(jnp.float32)
-    per_slow = top_wavenumber * bin_here / (lowest_bin + bin_count)
-
-    def coefficients(chunk, carry):
-        wavenumber = per_slow * slow_t[chunk]
-        squared = wavenumber * wavenumber
-        pairs = [node_value(squared, angle) for angle in NODE_ANGLES]
-        for comp in range(2):
-            found = project([pair[comp] for pair in pairs], list(range(NTERMS)), NODES)
-            for term in range(NTERMS):
-                coef[chunk, 2 * term + comp] = found[term]
-        return carry
-
-    lax.fori_loop(0, depths * chunks, coefficients, 0)
-
-    for copy in spec_copies:
-        copy.wait()
     for s in range(cores):
         for p in range(peers):
             group, inner = divmod(p * rows_here, SUBLANES)
@@ -208,6 +188,27 @@
                         s, p, c * rows_here : (c + 1) * rows_here, t * LANES : (t + 1) * LANES
                     ]
 
+    bin_here = (lowest_bin + me * cores + core).astype(jnp.float32)
+    per_slow = top_wavenumber * bin_here / (lowest_bin + bin_count)
+
+    def coefficients(z, chunk):
+        wavenumber = per_slow * slow_t[z * chunks + chunk]
+        squared = wavenumber * wavenumber
+        pairs = [node_value(squared, angle) for angle in NODE_ANGLES]
+        for comp in range(2):
+            found = project([pair[comp] for pair in pairs], list(range(NTERMS)), NODES)
+            for term in range(NTERMS):
+                coef[z][2 * term + comp, chunk] = found[term]
+
+    def all_coefficients(z):
+        if inline:
+            for chunk in range(chunks):
+                coefficients(z, chunk)
+        else:
+            lax.fori_loop(0, chunks, lambda chunk, carry: coefficients(z, chunk) or carry, 0)
+
+    all_coefficients(0)
+
     shape = (1, 1, 1, SUBLANES, LANES)
     lane = lax.broadcasted_iota(jnp.int32, shape, 4)
     row = lax.broadcasted_iota(jnp.int32, shape, 3)
@@ -217,9 +218,9 @@
     for z in range(depths):
 
         def term_of(current, n):
-            here = coef[z * chunks : (z + 1) * chunks, pl.ds(2 * n, 2)]
-            real_c = here[:, 0].reshape(groups, tiles, SUBLANES, LANES)
-            imag_c = here[:, 1].reshape(groups, tiles, SUBLANES, LANES)
+            here = coef[z][pl.ds(2 * n, 2)]
+            real_c = here[0].reshape(groups, tiles, SUBLANES, LANES)
+            imag_c = here[1].reshape(groups, tiles, SUBLANES, LANES)
             return jnp.stack(
                 [
                     real_c * current[0] - imag_c * current[1],
@@ -237,9 +238,17 @@
             following = spread_twice(current, lane, row) - (2.0 * current + previous)
             return current, following, total + term_of(following, n)
 
-        values = lax.fori_loop(
-            2, NTERMS, advance, (values, first, summed), unroll=groups <= 4
-        )[2]
+        state = (values, first, summed)
+        if inline:
+            for n in range(2, NTERMS):
+                state = advance(n, state)
+                if z + 1 < depths and n % 2 == 0 and n // 2 <= chunks:
+                    coefficients(z + 1, n // 2 - 1)
+        else:
+            state = lax.fori_loop(2, NTERMS, advance, state)
+            if z + 1 < depths:
+                all_coefficients(z + 1)
+        values = state[2]
         picture = values[0] * values[2] + values[1] * values[3]
         for group in range(groups):
             for t in range(tiles):
@@ -255,6 +264,8 @@
         copy.start()
         image_copies.append(copy)
         out_ref[core, z] = image[z, core]
+    for copy in spec_copies:
+        copy.wait_send()
     for copy in image_copies:
         copy.wait()
 
@@ -278,21 +289,18 @@
             pltpu.VMEM((tiles, length, rows_here, LANES), jnp.bfloat16),
             pltpu.VMEM(table.shape, jnp.bfloat16),
             pltpu.VMEM((depths, rows_here, cols), f32),
-            pltpu.VMEM((peers, depths, rows_here, cols), f32),
-            pltpu.VMEM((peers, cores, 2 * rows_here, cols), f32),
-            pltpu.VMEM((cores, peers, 2 * rows_here, cols), f32),
+            pltpu.VMEM((peers, cores, (2 + depths) * rows_here, cols), f32),
+            pltpu.VMEM((cores, peers, (2 + depths) * rows_here, cols), f32),
             pltpu.VMEM((depths * groups * tiles, SUBLANES, LANES), f32),
-            pltpu.VMEM((depths * groups * tiles, 2 * NTERMS, SUBLANES, LANES), f32),
             pltpu.VMEM((4, groups, tiles, SUBLANES, LANES), f32),
             pltpu.VMEM((depths, 2, grid_rows // 2, cols), f32),
             pltpu.SemaphoreType.DMA((2 + tiles,)),
-            pltpu.SemaphoreType.DMA((peers,)),
-            pltpu.SemaphoreType.DMA((peers,)),
             pltpu.SemaphoreType.DMA((others,)),
             pltpu.SemaphoreType.DMA((others,)),
             pltpu.SemaphoreType.DMA((depths,)),
             pltpu.SemaphoreType.DMA((depths,)),
-        ],
+        ]
+        + [pltpu.VMEM((2 * NTERMS, groups * tiles, SUBLANES, LANES), f32)] * depths,
         compiler_params=pltpu.CompilerParams(
             collective_id=0, has_side_effects=True, vmem_limit_bytes=64 * 1024 * 1024
         ),

time: 15.4 us -> 15.7 us (1.019)
  Pallas kernels: 13.8 us -> 14.1 us
    pallas_call x1, Pallas kernels: 13.8 us -> 14.1 us  [local(): pl.pallas_call(functools.partial(kernel, peers, cores, depths, rows_here,...]
where the time goes in v3:
time: 15.7 us; the launch traced here: 15.5 us
  Pallas kernels  14.1 us (90%)
  local copies, waits for them, and re-layouts  1.38 us (9%)
    pallas_call x1, Pallas kernels, local(): pl.pallas_call(functools.partial(kernel, peers, cores, depths, rows_here,...  14.1 us
    unnamed x1, local copies, waits for them, and re-layouts  1.38 us

profile of v3, /device:TPU:0, one launch (start us, length us, event | category | flops | bytes accessed | tf_op | source)
XLA Modules:
  0.0 15.5 jit_solution(4073576331118071712)
XLA Ops:
  0.0 14.1 %shard_map.37 = f32[2,2,8,256]{3,2,1,0:T(8,128)} custom-call(bf16[1024,2,256]{2,1,0:T(2,128)(2,1)} %bitcast.1, bf16[64,2048]{1,0:T(8,128)(2,1)} %constant.2.clone.table_ref, f32[2,2,256]{2,1,0:T(2,128)} %slow_ref.1), custom_call_target="tpu_custom_call" | custom-call | tf_op jit(solution)/shard_map/pallas_call | solution.py:283
  14.1 1.4 %copy.5 = f32[2,2,8,256]{3,2,1,0:T(8,128)} copy(f32[2,2,8,256]{3,2,1,0:T(8,128)} %shard_map.37) | data formatting | bytes 65536

commit v4 on v3

--- a/solution.py
+++ b/solution.py
@@ -13,6 +13,7 @@
 NODES = 16
 LANES = 128
 SUBLANES = 8
+PIECES = 4
 
 lowest_bin = 8
 top_wavenumber = 3.0
@@ -130,10 +131,11 @@
             device_id_type=pl.DeviceIdType.MESH,
         )
     loads = []
-    for t in range(tiles):
-        load = pltpu.make_async_copy(
-            traces_ref.at[:, :, pl.ds(t * LANES, LANES)], traces_v.at[t], load_sem.at[2 + t]
-        )
+    length = traces_v.shape[0]
+    piece = length // PIECES
+    for t in range(PIECES):
+        span = pl.ds(t * piece, piece)
+        load = pltpu.make_async_copy(traces_ref.at[span], traces_v.at[span], load_sem.at[2 + t])
         load.start()
         loads.append(load)
     load_table = pltpu.make_async_copy(table_ref, table_v, load_sem.at[1])
@@ -144,17 +146,19 @@
     load_slow.wait()
     slow_rows = own_slow[...].reshape(depths * rows_here, cols)
     tail = jnp.concatenate([jnp.zeros((spec_rows, cols), jnp.float32), slow_rows], axis=0)
-    block_row = lax.broadcasted_iota(jnp.int32, (1, 1, 2 * spec_rows, LANES), 2)
+    block_row = lax.broadcasted_iota(jnp.int32, (1, 1, 2 * spec_rows, cols), 2)
     load_table.wait()
-    length = traces_v.shape[1]
-    for t in range(tiles):
+    part = jnp.zeros((bin_count * spec_rows, cols), jnp.float32)
+    for t in range(PIECES):
         loads[t].wait()
-        block = traces_v[t].reshape(length * rows_here, LANES)
-        part = jnp.dot(table_v[...], block, preferred_element_type=jnp.float32)
-        part = part.reshape(peers, 1, cores * spec_rows, LANES)
-        both = jnp.concatenate([part, pltpu.roll(part, spec_rows, 2)], axis=1)
-        here = tail[:, t * LANES : (t + 1) * LANES]
-        send[:, :, :, t * LANES : (t + 1) * LANES] = jnp.where(block_row < spec_rows, both, here[None, None])
+        width = piece * rows_here
+        block = traces_v[t * piece : (t + 1) * piece].reshape(width, cols)
+        part = part + jnp.dot(
+            table_v[:, t * width : (t + 1) * width], block, preferred_element_type=jnp.float32
+        )
+    part = part.reshape(peers, 1, cores * spec_rows, cols)
+    both = jnp.concatenate([part, pltpu.roll(part, spec_rows, 2)], axis=1)
+    send[...] = jnp.where(block_row < spec_rows, both, tail[None, None])
 
     pl.semaphore_wait(barrier, len(others))
     spec_copies = []
@@ -286,7 +290,7 @@
         in_specs=[pl.BlockSpec(memory_space=pltpu.HBM)] * 3,
         out_specs=pl.BlockSpec(memory_space=pltpu.VMEM),
         scratch_shapes=[
-            pltpu.VMEM((tiles, length, rows_here, LANES), jnp.bfloat16),
+            pltpu.VMEM((length, rows_here, cols), jnp.bfloat16),
             pltpu.VMEM(table.shape, jnp.bfloat16),
             pltpu.VMEM((depths, rows_here, cols), f32),
             pltpu.VMEM((peers, cores, (2 + depths) * rows_here, cols), f32),
@@ -294,7 +298,7 @@
             pltpu.VMEM((depths * groups * tiles, SUBLANES, LANES), f32),
             pltpu.VMEM((4, groups, tiles, SUBLANES, LANES), f32),
             pltpu.VMEM((depths, 2, grid_rows // 2, cols), f32),
-            pltpu.SemaphoreType.DMA((2 + tiles,)),
+            pltpu.SemaphoreType.DMA((2 + PIECES,)),
             pltpu.SemaphoreType.DMA((others,)),
             pltpu.SemaphoreType.DMA((others,)),
             pltpu.SemaphoreType.DMA((depths,)),

time: 15.7 us -> 15.6 us (level)
  no operation moved by 1% of the time
where the time goes in v4:
time: 15.6 us; the launch traced here: 15.4 us
  Pallas kernels  14.1 us (90%)
  local copies, waits for them, and re-layouts  1.38 us (9%)
    pallas_call x1, Pallas kernels, local(): pl.pallas_call(functools.partial(kernel, peers, cores, depths, rows_here,...  14.1 us
    unnamed x1, local copies, waits for them, and re-layouts  1.38 us

profile of v4, /device:TPU:0, one launch (start us, length us, event | category | flops | bytes accessed | tf_op | source)
XLA Modules:
  0.0 15.4 jit_solution(578358138216239690)
XLA Ops:
  0.0 14.1 %shard_map.37 = f32[2,2,8,256]{3,2,1,0:T(8,128)} custom-call(bf16[1024,2,256]{2,1,0:T(2,128)(2,1)} %bitcast.1, bf16[64,2048]{1,0:T(8,128)(2,1)} %constant.2.clone.table_ref, f32[2,2,256]{2,1,0:T(2,128)} %slow_ref.1), custom_call_target="tpu_custom_call" | custom-call | tf_op jit(solution)/shard_map/pallas_call | solution.py:287
  14.1 1.4 %copy.5 = f32[2,2,8,256]{3,2,1,0:T(8,128)} copy(f32[2,2,8,256]{3,2,1,0:T(8,128)} %shard_map.37) | data formatting | bytes 65536
